TPU v7x, 32 devices: a whole 2x2x4 slice. The times are simulated.
32 devices in a mesh: fsdp: 4 (over y, x), seq: 4 (over z), head: 2 (over core).
Axes of the slice: x: 2, y: 2, z: 4, core: 2. Of those that a mesh axis runs over, the one named last changes fastest.
Arguments:
- hidden: bfloat16 [8, 1024, 1024], P('fsdp', 'seq'), may hold values from -6 to 6
- segment_ids: int32 [8, 1024], P('fsdp'), may hold values from 0 to 6, as said below
- norm_gain: float32 [1024], replicated, may hold values from 0.5 to 1.5
- w_zx: bfloat16 [1024, 2, 2048], P('fsdp', None, 'head'), may hold values from -0.1875 to 0.1875
- w_bcdt: bfloat16 [1024, 288], P('fsdp'), may hold values from -0.1875 to 0.1875
- conv_x: float32 [4, 2048], P(None, 'head'), may hold values from -3 to 3
- conv_x_bias: float32 [2048], P('head'), may hold values from -0.5 to 0.5
- conv_bc: float32 [4, 256], replicated, may hold values from -3 to 3
- conv_bc_bias: float32 [256], replicated, may hold values from -0.5 to 0.5
- dt_bias: float32 [32], P('head'), may hold values from -7 to -2
- a_log: float32 [32], P('head'), may hold values from 0 to 2.7
- d_skip: float32 [32], P('head'), may hold values from 0.5 to 1.5
- gate_gain: float32 [2048], P('head'), may hold values from 0.5 to 1.5
- w_out: bfloat16 [2048, 1024], P('head', 'fsdp'), may hold values from -0.125 to 0.125
- cotangent: bfloat16 [8, 1024, 1024], P('fsdp', 'seq'), may hold values from -6 to 6
Outputs:
- block_out: bfloat16 [8, 1024, 1024], P('fsdp', 'seq')
- grad_hidden: float32 [8, 1024, 1024], P('fsdp', 'seq')
- grad_norm_gain: float32 [1024], replicated
- grad_w_zx: float32 [1024, 2, 2048], P('fsdp', None, 'head')
- grad_w_bcdt: float32 [1024, 288], P('fsdp')
- grad_conv_x: float32 [4, 2048], P(None, 'head')
- grad_conv_x_bias: float32 [2048], P('head')
- grad_conv_bc: float32 [4, 256], replicated
- grad_conv_bc_bias: float32 [256], replicated
- grad_dt_bias: float32 [32], P('head')
- grad_a_log: float32 [32], P('head')
- grad_d_skip: float32 [32], P('head')
- grad_gate_gain: float32 [2048], P('head')
- grad_w_out: float32 [2048, 1024], P('head', 'fsdp')
Inputs may be any that keep to these rules, and one draw needn't show every extreme that they name: `segment_ids`: within a sequence the ids count its documents from 0 and never fall; whole documents hold 204 to 2048 tokens, the first and last cut by the sequence's ends; among the 2 sequences of each index of fsdp one is a single document.
All inputs are finite; a program needn't handle non-finite values.
Results may differ from a plain program's by a relative error of at most 0.012.
The roundings to bfloat16 on the way count: a program that leaves them out, or rounds other values in their place, can miss the bound.
Values may be sent and summed in bfloat16 or wider, within the bound.
No kernel may reach another device: no remote copies, remote signals or barrier semaphores. Data moves between devices by JAX's collectives and lax.ppermute only.
A program may use at most 192 MiB of HBM per device.

v0:
```python
import jax
import jax.numpy as jnp
from jax import lax
from jax.sharding import PartitionSpec as P

P_SIZE = 64
N = 128
NH = 32
KC = 4
MB = 2
NBC = 288


EPS = 1e-05
MIXED = lax.Precision.HIGH


def passed_along(value, axis, steps):
    count = lax.axis_size(axis)
    initial, last = (max(0, -steps), min(count, count - steps))
    return lax.ppermute(value, axis, [(source, source + steps) for source in range(initial, last)])


def entering(part, axis, combine, identity, reverse):
    count = lax.axis_size(axis)
    place = lax.axis_index(axis)
    ahead = count - 1 - place if reverse else place
    gathered = jax.tree.map(lambda a: lax.all_gather(a, axis), part)
    state = jax.tree.map(lambda a, e: jnp.zeros_like(a) + jnp.asarray(e, a.dtype), part, identity)

    def one(lap, state):
        source = count - 1 - lap if reverse else lap
        return combine(
            state, jax.tree.map(lambda a: lax.dynamic_index_in_dim(a, source, 0, False), gathered)
        )

    return lax.fori_loop(0, ahead, one, state)


def conv_layer(extended, conv_weight, conv_bias, seg_wide):
    run_rows = extended.shape[-2] - (KC - 1)
    own_seg = seg_wide[..., KC - 1 :]
    pre_act = (
        jnp.zeros(extended.shape[:-2] + (run_rows, extended.shape[-1]), jnp.float32) + conv_bias
    )
    for tap_index in range(KC):
        same_seg = (seg_wide[..., tap_index : tap_index + run_rows] == own_seg).astype(jnp.float32)
        pre_act = (
            pre_act
            + conv_weight[tap_index]
            * extended[..., tap_index : tap_index + run_rows, :]
            * same_seg[..., None]
        )
    return pre_act * jax.nn.sigmoid(pre_act)


def ssd_span(
    ssm_state, x_heads, b_rows, c_rows, dt_rows, seg_rows, seg_prev, decay_rate, skip_gain
):
    block_len = x_heads.shape[0]
    log_decay = jnp.cumsum(dt_rows * decay_rate, axis=0)
    decay_heads = log_decay.T
    dt_heads = dt_rows.T
    positions = jnp.arange(block_len)
    keep_mask = (positions[:, None] >= positions[None, :]) & (
        seg_rows[:, None] == seg_rows[None, :]
    )
    keep_wide = keep_mask[None, :, :]
    log_gap = jnp.where(keep_wide, decay_heads[:, :, None] - decay_heads[:, None, :], 0.0)
    decay_mat = jnp.where(keep_wide, jnp.exp(log_gap), 0.0)
    c_dot_b = jnp.dot(c_rows, b_rows.T, precision=MIXED)
    mix_mat = c_dot_b[None, :, :] * decay_mat * dt_heads[:, None, :]
    y_block = jnp.einsum("hts,shp->thp", mix_mat, x_heads, precision=MIXED)
    entry_gain = jnp.where((seg_rows == seg_prev)[:, None], jnp.exp(log_decay), 0.0)
    y_block = y_block + entry_gain[:, :, None] * jnp.einsum(
        "tn,hpn->thp", c_rows, ssm_state, precision=MIXED
    )
    y_block = y_block + skip_gain[None, :, None] * x_heads
    tail_gain = (
        jnp.where(
            (seg_rows == seg_rows[-1])[:, None], jnp.exp(log_decay[-1][None, :] - log_decay), 0.0
        )
        * dt_rows
    )
    fresh_state = jnp.einsum(
        "shp,sn->hpn", tail_gain[:, :, None] * x_heads, b_rows, precision=MIXED
    )
    span_gain = jnp.where(seg_rows[-1] == seg_prev, jnp.exp(log_decay[-1]), 0.0)
    return (span_gain[:, None, None] * ssm_state + fresh_state, y_block)


def ssd_run(x_heads, b_rows, c_rows, dt_raw, dt_bias, a_log, d_skip, seg_rows, seg_prev, ssm_state):
    dt_rows = jax.nn.softplus(dt_raw + dt_bias)
    decay_rate = -jnp.exp(a_log)
    ssm_state, y_block = ssd_span(
        ssm_state, x_heads, b_rows, c_rows, dt_rows, seg_rows, seg_prev, decay_rate, d_skip
    )
    y_parts = [y_block]
    return (jnp.concatenate(y_parts, axis=0), ssm_state)


def entry_terms(dt_raw, dt_bias, a_log, seg_rows, seg_prev):
    log_decay = jnp.cumsum(jax.nn.softplus(dt_raw + dt_bias) * -jnp.exp(a_log), axis=1)
    entry_gain = jnp.where((seg_rows == seg_prev[:, None])[:, :, None], jnp.exp(log_decay), 0.0)
    run_gain = jnp.where((seg_rows[:, -1] == seg_prev)[:, None], jnp.exp(log_decay[:, -1]), 0.0)
    return (entry_gain, run_gain)


def combine(earlier, later):
    return (earlier[0] * later[0], later[0] * earlier[1] + later[1])


def shards(
    hidden,
    segment_ids,
    norm_gain,
    w_zx,
    w_bcdt,
    conv_x,
    conv_x_bias,
    conv_bc,
    conv_bc_bias,
    dt_bias,
    a_log,
    d_skip,
    gate_gain,
    w_out,
    cotangent,
):
    head_count = lax.axis_size("head")
    head_place = lax.axis_index("head")
    seq_place = lax.axis_index("seq")
    seq_count, run_rows, model_width = hidden.shape
    inner_local = w_zx.shape[2]
    heads_local = dt_bias.shape[0]
    inner_full = inner_local * head_count
    group_size = seq_count // MB
    run_start = seq_place * run_rows
    seg_padded = jnp.concatenate(
        [jnp.full((seq_count, KC - 1), -1, jnp.int32), segment_ids], axis=1
    )
    seg_wide = lax.dynamic_slice_in_dim(seg_padded, run_start, run_rows + KC - 1, 1)
    seg_run = seg_wide[:, KC - 1 :]
    seg_before = seg_wide[:, KC - 2]
    conv_weight = jnp.concatenate([conv_x, conv_bc], axis=1)
    conv_bias = jnp.concatenate([conv_x_bias, conv_bc_bias])
    scan_unit = (
        jnp.ones((group_size, heads_local, 1, 1), jnp.float32),
        jnp.zeros((group_size, heads_local, P_SIZE, N), jnp.float32),
    )
    batched_run = jax.vmap(ssd_run, in_axes=(0, 0, 0, 0, None, None, None, 0, 0, 0))
    saved = []
    outputs = []
    for micro in range(MB):
        gathered = (
            lax.all_gather(w_zx, "fsdp", axis=0, tiled=True),
            lax.all_gather(w_bcdt, "fsdp", axis=0, tiled=True),
            lax.all_gather(w_out, "fsdp", axis=1, tiled=True),
        )
        zx_full, bcdt_full, out_full = gathered
        zx_flat = zx_full.reshape(model_width, 2 * inner_local)
        lower = micro * group_size
        upper = lower + group_size
        part_hidden = hidden[lower:upper].astype(jnp.float32)
        inv_rms = lax.rsqrt(jnp.mean(part_hidden * part_hidden, axis=-1, keepdims=True) + EPS)
        normed = (part_hidden * inv_rms * norm_gain).astype(jnp.bfloat16).reshape(-1, model_width)
        zx_proj = (
            jnp.dot(normed, zx_flat, preferred_element_type=jnp.float32)
            .astype(jnp.bfloat16)
            .reshape(group_size, run_rows, 2 * inner_local)
        )
        bcdt_proj = (
            jnp.dot(normed, bcdt_full, preferred_element_type=jnp.float32)
            .astype(jnp.bfloat16)
            .reshape(group_size, run_rows, NBC)
        )
        z_gate = zx_proj[..., :inner_local].astype(jnp.float32)
        xbc_pre = jnp.concatenate([zx_proj[..., inner_local:], bcdt_proj[..., : 2 * N]], axis=-1)
        dt_raw = lax.dynamic_slice_in_dim(
            bcdt_proj[..., 2 * N :], head_place * heads_local, heads_local, 2
        ).astype(jnp.float32)
        rim_rows = passed_along(xbc_pre[:, run_rows - (KC - 1) :], "seq", 1)
        extended = jnp.concatenate([rim_rows, xbc_pre], axis=1).astype(jnp.float32)
        seg_group = seg_wide[lower:upper]
        conv_out = conv_layer(extended, conv_weight, conv_bias, seg_group).astype(jnp.bfloat16)
        x_heads = (
            conv_out[..., :inner_local]
            .astype(jnp.float32)
            .reshape(group_size, run_rows, heads_local, P_SIZE)
        )
        b_rows = conv_out[..., inner_local : inner_local + N].astype(jnp.float32)
        c_rows = conv_out[..., inner_local + N :].astype(jnp.float32)
        seg_last = seg_before[lower:upper]
        seg_local = seg_run[lower:upper]
        y_local, state_local = batched_run(
            x_heads,
            b_rows,
            c_rows,
            dt_raw,
            dt_bias,
            a_log,
            d_skip,
            seg_local,
            seg_last,
            scan_unit[1],
        )
        entry_gain, run_gain = entry_terms(dt_raw, dt_bias, a_log, seg_local, seg_last)
        run_gain = run_gain[:, :, None, None]
        state_in = entering((run_gain, state_local), "seq", combine, scan_unit, False)[1]
        y_heads = y_local + entry_gain[..., None] * jnp.einsum(
            "grn,ghpn->grhp", c_rows, state_in, precision=MIXED
        )
        y_flat = y_heads.reshape(group_size, run_rows, inner_local)
        gate_sig = jax.nn.sigmoid(z_gate)
        gated = y_flat * z_gate * gate_sig
        square_sum = lax.psum(jnp.sum(gated * gated, axis=-1), "head")
        gate_rms = lax.rsqrt(square_sum / inner_full + EPS)[..., None]
        out_norm = (gated * gate_rms * gate_gain).astype(jnp.bfloat16).reshape(-1, inner_local)
        partial_out = jnp.dot(out_norm, out_full, preferred_element_type=jnp.float32)
        mixed = lax.psum(partial_out, "head").reshape(group_size, run_rows, model_width)
        outputs.append((part_hidden + mixed).astype(jnp.bfloat16))
        saved.append(
            (
                part_hidden,
                inv_rms,
                normed,
                z_gate,
                gate_sig,
                extended,
                seg_group,
                dt_raw,
                x_heads,
                b_rows,
                c_rows,
                seg_local,
                seg_last,
                state_in,
                entry_gain,
                run_gain,
                y_flat,
                gated,
                gate_rms,
                out_norm,
            )
        )
    grad_zx = jnp.zeros((model_width, 2 * inner_local), jnp.float32)
    grad_bcdt = jnp.zeros((model_width, NBC), jnp.float32)
    grad_out = jnp.zeros((inner_local, model_width), jnp.float32)
    grad_norm = jnp.zeros((model_width,), jnp.float32)
    grad_conv = jnp.zeros_like(conv_weight)
    grad_conv_bias = jnp.zeros_like(conv_bias)
    grad_dtb = jnp.zeros((heads_local,), jnp.float32)
    grad_alog = jnp.zeros((heads_local,), jnp.float32)
    grad_skip = jnp.zeros((heads_local,), jnp.float32)
    grad_gate = jnp.zeros((inner_local,), jnp.float32)
    input_grads = [None] * MB
    for micro in reversed(range(MB)):
        gathered = (
            lax.all_gather(w_zx, "fsdp", axis=0, tiled=True),
            lax.all_gather(w_bcdt, "fsdp", axis=0, tiled=True),
            lax.all_gather(w_out, "fsdp", axis=1, tiled=True),
        )
        zx_full, bcdt_full, out_full = gathered
        zx_flat = zx_full.reshape(model_width, 2 * inner_local)
        (
            part_hidden,
            inv_rms,
            normed,
            z_gate,
            gate_sig,
            extended,
            seg_group,
            dt_raw,
            x_heads,
            b_rows,
            c_rows,
            seg_local,
            seg_last,
            state_in,
            entry_gain,
            run_gain,
            y_flat,
            gated,
            gate_rms,
            out_norm,
        ) = saved[micro]
        lower = micro * group_size
        upper = lower + group_size
        cot_flat = cotangent[lower:upper].reshape(-1, model_width)
        grad_out = grad_out + jnp.einsum(
            "ti,td->id", out_norm, cot_flat, preferred_element_type=jnp.float32
        )
        d_outn = jnp.einsum(
            "td,id->ti", cot_flat, out_full, preferred_element_type=jnp.float32
        ).reshape(group_size, run_rows, inner_local)
        grad_gate = grad_gate + jnp.sum(d_outn * gated * gate_rms, axis=(0, 1))
        scaled = d_outn * gate_gain
        cross_sum = lax.psum(jnp.sum(scaled * gated, axis=-1), "head")
        d_gated = scaled * gate_rms - gated * gate_rms**3 * cross_sum[..., None] / inner_full
        d_y = (d_gated * z_gate * gate_sig).reshape(group_size, run_rows, heads_local, P_SIZE)
        d_z = d_gated * y_flat * gate_sig * (1.0 + z_gate * (1.0 - gate_sig))
        local_back = jnp.einsum("grh,grhp,grn->ghpn", entry_gain, d_y, c_rows, precision=MIXED)
        state_out = entering((run_gain, local_back), "seq", combine, scan_unit, True)[1]

        def ssd_piece(x_in, b_in, c_in, dt_in, bias_in, alog_in, skip_in):
            return batched_run(
                x_in, b_in, c_in, dt_in, bias_in, alog_in, skip_in, seg_local, seg_last, state_in
            )

        _, ssd_pull = jax.vjp(ssd_piece, x_heads, b_rows, c_rows, dt_raw, dt_bias, a_log, d_skip)
        d_x, d_b, d_c, d_dt, d_bias, d_alog, d_skipg = ssd_pull((d_y, state_out))
        grad_dtb = grad_dtb + d_bias
        grad_alog = grad_alog + d_alog
        grad_skip = grad_skip + d_skipg
        dt_wide = lax.dynamic_update_slice_in_dim(
            jnp.zeros((group_size, run_rows, NH), jnp.float32), d_dt, head_place * heads_local, 2
        )
        d_bc, dt_wide = lax.psum((jnp.concatenate([d_b, d_c], axis=-1), dt_wide), "head")
        d_act = jnp.concatenate([d_x.reshape(group_size, run_rows, inner_local), d_bc], axis=-1)

        def conv_piece(ext_in, weight_in, bias_in):
            return conv_layer(ext_in, weight_in, bias_in, seg_group)

        _, conv_pull = jax.vjp(conv_piece, extended, conv_weight, conv_bias)
        d_ext, d_weight, d_cbias = conv_pull(d_act)
        grad_conv = grad_conv + d_weight
        grad_conv_bias = grad_conv_bias + d_cbias
        rim_back = passed_along(d_ext[:, : KC - 1], "seq", -1)
        d_xbc = d_ext[:, KC - 1 :] + jnp.concatenate(
            [jnp.zeros((group_size, run_rows - (KC - 1), d_ext.shape[2]), jnp.float32), rim_back],
            axis=1,
        )
        d_zx = (
            jnp.concatenate([d_z, d_xbc[..., :inner_local]], axis=-1)
            .astype(jnp.bfloat16)
            .reshape(-1, 2 * inner_local)
        )
        d_bcdt = (
            jnp.concatenate([d_xbc[..., inner_local:], dt_wide], axis=-1)
            .astype(jnp.bfloat16)
            .reshape(-1, NBC)
        )
        grad_zx = grad_zx + jnp.einsum(
            "td,tc->dc", normed, d_zx, preferred_element_type=jnp.float32
        )
        grad_bcdt = grad_bcdt + jnp.einsum(
            "td,tc->dc", normed, d_bcdt, preferred_element_type=jnp.float32
        )
        zx_back = jnp.einsum("tc,dc->td", d_zx, zx_flat, preferred_element_type=jnp.float32)
        d_normed = lax.psum(zx_back, "head") + jnp.einsum(
            "tc,dc->td", d_bcdt, bcdt_full, preferred_element_type=jnp.float32
        )
        d_normed = d_normed.reshape(group_size, run_rows, model_width)
        grad_norm = grad_norm + jnp.sum(d_normed * part_hidden * inv_rms, axis=(0, 1))
        scaled_in = d_normed * norm_gain
        input_grads[micro] = (
            cotangent[lower:upper].astype(jnp.float32)
            + scaled_in * inv_rms
            - part_hidden
            * inv_rms**3
            * jnp.sum(scaled_in * part_hidden, axis=-1, keepdims=True)
            / model_width
        )
    grad_zx, grad_bcdt, grad_out = (
        lax.psum_scatter(
            grad_zx.reshape(model_width, 2, inner_local), "fsdp", scatter_dimension=0, tiled=True
        ),
        lax.psum_scatter(grad_bcdt, "fsdp", scatter_dimension=0, tiled=True),
        lax.psum_scatter(grad_out, "fsdp", scatter_dimension=1, tiled=True),
    )
    grad_zx, grad_bcdt, grad_out = lax.psum((grad_zx, grad_bcdt, grad_out), "seq")
    small_sums = lax.psum(
        (grad_norm, grad_conv, grad_conv_bias, grad_dtb, grad_alog, grad_skip, grad_gate),
        ("fsdp", "seq"),
    )
    grad_norm, grad_conv, grad_conv_bias, grad_dtb, grad_alog, grad_skip, grad_gate = small_sums
    return (
        jnp.concatenate(outputs, axis=0),
        jnp.concatenate(input_grads, axis=0),
        grad_norm,
        grad_zx,
        grad_bcdt,
        grad_conv[:, :inner_local],
        grad_conv_bias[:inner_local],
        grad_conv[:, inner_local:],
        grad_conv_bias[inner_local:],
        grad_dtb,
        grad_alog,
        grad_skip,
        grad_gate,
        grad_out,
    )


def solution(mesh):
    placed = (
        P("fsdp", "seq", None),
        P("fsdp", None),
        P(),
        P("fsdp", None, "head"),
        P("fsdp", None),
        P(None, "head"),
        P("head"),
        P(),
        P(),
        P("head"),
        P("head"),
        P("head"),
        P("head"),
        P("head", "fsdp"),
        P("fsdp", "seq", None),
    )
    return jax.shard_map(
        shards,
        mesh=mesh,
        in_specs=placed,
        out_specs=(
            P("fsdp", "seq", None),
            P("fsdp", "seq", None),
            P(),
            P("fsdp", None, "head"),
            P("fsdp", None),
            P(None, "head"),
            P("head"),
            P(),
            P(),
            P("head"),
            P("head"),
            P("head"),
            P("head"),
            P("head", "fsdp"),
        ),
        check_vma=False,
    )
```

profile of v0, /device:TPU:0, one launch (start us, length us, event | category | flops | bytes accessed | tf_op | source)
XLA Modules:
  0.0 843.6 jit_solution(3386475326015250923)
XLA Ops:
  9.0 19.8 %all_gather.51 = bf16[1024,288]{0,1:T(8,128)(2,1)S(1)} all-gather(bf16[256,288]{0,1:T(8,128)(2,1)S(1)} %copy-done.64), channel_id=1, replica_groups=mesh['fsdp'=4,'seq'=4,'head'=2] {'fsdp'}, dimensions={0}, use_global_device_ids=true | all-gather | bytes 737280 | tf_op jit(solution)/shard_map/all_gather | solution.py:157
  46.9 20.2 %all-gather.13.cloned.1.call-done = bf16[1024,2,1024]{2,1,0:T(2,128)(2,1)} async-done(((bf16[256,2,1024]{2,1,0:T(2,128)(2,1)}), bf16[1024,2,1024]{2,1,0:T(2,128)(2,1)}) %all-gather.13.cloned.1.call-update) | async-done | bytes 4194320 | tf_op jit(solution)/shard_map/all_gather | solution.py:156
  96.5 10.1 %all-gather = f32[4,1,16]{2,1,0:T(1,128)S(1)} all-gather(f32[1,1,16]{2,1,0:T(1,128)S(1)} %copy.432), channel_id=2, replica_groups=mesh['fsdp'=4,'seq'=4,'head'=2] {'seq'}, dimensions={0}, use_global_device_ids=true | all-gather | bytes 320 | tf_op jit(solution)/shard_map/all_gather | solution.py:28
  106.6 8.0 all-gather.2
  145.0 6.5 all-gather.17.cloned.1.call-done
  153.2 4.9 fusion.73
  163.4 34.1 %all-gather.19.cloned.1.call-done = f32[64,64,128]{2,1,0:T(8,128)} async-done(((f32[16,64,128]{2,1,0:T(8,128)}), f32[64,64,128]{2,1,0:T(8,128)}) %all-gather.19.cloned.1.call-update) | async-done | bytes 2097168 | tf_op jit(solution)/shard_map/all_gather | solution.py:28
  200.1 4.9 fusion.64
  212.7 5.3 fusion.131
  220.4 6.0 multiply_reduce_fusion.12
  254.7 6.3 fusion.17
  263.0 6.4 fusion.19
  276.8 6.2 all-gather.21.cloned.1.call-done
  283.9 8.4 while.54
  295.2 34.0 %all-gather.23.cloned.1.call-done = f32[64,64,128]{2,1,0:T(8,128)} async-done(((f32[16,64,128]{2,1,0:T(8,128)}), f32[64,64,128]{2,1,0:T(8,128)}) %all-gather.23.cloned.1.call-update) | async-done | bytes 2097168 | tf_op jit(solution)/shard_map/all_gather | solution.py:28
  330.0 8.4 while.55
  353.7 5.3 fusion.76
  387.4 11.7 %reshape.1717 = f32[1024,2,1024]{2,1,0:T(2,128)} reshape(f32[1024,2048]{1,0:T(8,128)} %convolution_add_fusion) | data formatting | bytes 16777216 | tf_op jit(solution)/shard_map/reshape | solution.py:366
  439.5 132.8 %all-reduce.36.cloned.1.call-done = f32[1024,2,1024]{2,1,0:T(2,128)} async-done(((f32[1024,2,1024]{2,1,0:T(2,128)}), f32[1024,2,1024]{2,1,0:T(2,128)}) %all-reduce.36.cloned.1.call-update) | async-done | bytes 8388624
  575.9 29.1 %reduce-scatter.3.cloned.1.call-done = f32[256,288]{0,1:T(8,128)} async-done(((f32[1024,288]{0,1:T(8,128)}), f32[256,288]{0,1:T(8,128)}) %reduce-scatter.3.cloned.1.call-update) | async-done | bytes 294928 | tf_op jit(solution)/shard_map/reduce_scatter | solution.py:368
  605.0 55.5 %reduce-scatter.5.cloned.1.call-done = f32[1024,256]{1,0:T(8,128)} async-done(((f32[1024,1024]{1,0:T(8,128)}), f32[1024,256]{1,0:T(8,128)}) %reduce-scatter.5.cloned.1.call-update) | async-done | bytes 1048592 | tf_op jit(solution)/shard_map/reduce_scatter | solution.py:369
  662.0 31.5 %all-reduce.40.cloned.1.call-done = (f32[1,256,1024]{2,1,0:T(8,128)}, f32[1,256,1024]{2,1,0:T(8,128)}, f32[256,1024]{1,0:T(8,128)}, f32[256,1024]{1,0:T(8,128)}) async-done(((f32[1,256,1024]{2,1,0:T(8,128)}, f32[1,256,1024]{2,1,0:T(8,128)}, f32[256,1024]{1,0:T(8,128)}, f32[256,1024]{1,0:T(8,128)}), (f32[1,256,1024]{2,1,0:T(8,128)}, f32[1,256,1024]{2,1,0:T(8,128)}, f32[256,1024]{1,0:T(8,128)}, ...) | async-done | bytes 4194320 | tf_op jit(solution)/shard_map/psum | solution.py:220
  697.3 81.7 %all-reduce.24 = (f32[1024]{0:T(1024)}, f32[4,1280]{1,0:T(4,128)S(1)}, f32[1280]{0:T(1024)S(1)}, f32[16]{0:T(128)}, f32[16]{0:T(128)}, /*index=5*/f32[16]{0:T(128)}, f32[1024]{0:T(1024)}) all-reduce(f32[1024]{0:T(1024)S(1)} %add.438, f32[4,1280]{1,0:T(4,128)S(1)} %add_add_fusion, ...), channel_id=1, replica_groups=mesh['fsdp'=4,'seq'=4,'head'=2] {'fsdp','seq'}, use_global_device_ids=true, to_apply=%region_58.60 | all-reduce | flops 8496 | bytes 67968 | tf_op jit(solution)/shard_map/psum | solution.py:372
  786.5 44.3 %all-reduce.38.cloned.1.call-done = (f32[256,2,1024]{2,1,0:T(2,128)}, f32[256,288]{0,1:T(8,128)}, f32[1024,256]{1,0:T(8,128)}) async-done(((f32[256,2,1024]{2,1,0:T(2,128)}, f32[256,288]{0,1:T(8,128)}, f32[1024,256]{1,0:T(8,128)}), (f32[256,2,1024]{2,1,0:T(2,128)}, f32[256,288]{0,1:T(8,128)}, f32[1024,256]{1,0:T(8,128)})) %all-reduce.38.cloned.1.call-update) | async-done | bytes 3440656 | tf_op jit(solution)/shard_map/psum | solution.py:371
  (611 shorter events, 258.6 us)
Async XLA Ops:
  7.2 59.9 %all-gather.13.cloned.1.call-start = ((), (), s32[]{:S(2)}) async-start(), calls=%async_computation.2 | async-start | bytes 5242880 | tf_op jit(solution)/shard_map/all_gather | solution.py:156
  7.9 108.0 %all-gather.15.cloned.1.call-start = ((), (), s32[]{:S(2)}) async-start(), calls=%async_computation.3 | async-start | bytes 2621440 | tf_op jit(solution)/shard_map/all_gather | solution.py:158
  8.7 142.9 %all-gather.17.cloned.1.call-start = ((), (), s32[]{:S(2)}) async-start(), calls=%async_computation.6 | async-start | bytes 2621440 | tf_op jit(solution)/shard_map/all_gather | solution.py:28
  31.5 50.4 %copy-start.68 = (f32[1280]{0:T(1024)}, f32[1280]{0:T(1024)S(1)}, u32[]{:S(2)}) copy-start(f32[1280]{0:T(1024)S(1)} %get-tuple-element.433) | copy-start | bytes 15364
  31.5 50.4 %copy-start.70 = (f32[1280]{0:T(1024)}, f32[1280]{0:T(1024)S(1)}, u32[]{:S(2)}) copy-start(f32[1280]{0:T(1024)S(1)} %get-tuple-element.434) | copy-start | bytes 15364
  72.1 8.3 collective-permute-start.1
  77.0 4.8 collective-permute-start
  85.5 58.7 %copy-start.12 = (bf16[1,256,1280]{2,1,0:T(8,128)(2,1)}, bf16[1,256,1280]{2,1,0:T(8,128)(2,1)S(1)}, u32[]{:S(2)}) copy-start(bf16[1,256,1280]{2,1,0:T(8,128)(2,1)S(1)} %get-tuple-element.552) | copy-start | bytes 1966084
  92.6 105.0 %all-gather.19.cloned.1.call-start = ((), (), s32[]{:S(2)}) async-start(), calls=%async_computation.7 | async-start | bytes 2621440 | tf_op jit(solution)/shard_map/all_gather | solution.py:28
  115.1 85.0 %copy-start.121 = (f32[16,256]{1,0:T(8,128)}, f32[16,256]{1,0:T(8,128)S(1)}, u32[]{:S(2)}) copy-start(f32[16,256]{1,0:T(8,128)S(1)} %bitcast_add_fusion.6) | copy-start | bytes 49156
  115.9 84.2 %copy-start.80 = (pred[256,256]{1,0:T(8,128)(4,1)}, pred[256,256]{1,0:T(8,128)(4,1)S(1)}, u32[]{:S(2)}) copy-start(pred[256,256]{1,0:T(8,128)(4,1)S(1)} %fusion.174) | copy-start | bytes 196612
  129.4 153.6 %all-gather.21.cloned.1.call-start = ((), (), s32[]{:S(2)}) async-start(), calls=%async_computation.8 | async-start | bytes 2621440 | tf_op jit(solution)/shard_map/all_gather | solution.py:28
  231.5 97.6 %all-gather.23.cloned.1.call-start = ((), (), s32[]{:S(2)}) async-start(), calls=%async_computation.9 | async-start | bytes 2621440 | tf_op jit(solution)/shard_map/all_gather | solution.py:28
  261.1 104.1 %all-reduce.42.cloned.1.call-start = ((), (), s32[]{:S(2)}) async-start(), calls=%async_computation.13 | async-start | bytes 1048576 | tf_op jit(solution)/shard_map/psum | solution.py:318
  348.2 224.1 %all-reduce.36.cloned.1.call-start = ((), (), s32[]{:S(2)}) async-start(), calls=%async_computation.10 | async-start | bytes 16777216
  372.3 5.7 collective-permute-start.3
  374.0 6.3 collective-permute-start.2
  399.2 205.9 %reduce-scatter.3.cloned.1.call-start = ((), (), s32[]{:S(2)}) async-start(), calls=%async_computation.4 | async-start | bytes 1474560 | tf_op jit(solution)/shard_map/reduce_scatter | solution.py:368
  421.0 239.5 %reduce-scatter.5.cloned.1.call-start = ((), (), s32[]{:S(2)}) async-start(), calls=%async_computation.5 | async-start | bytes 5242880 | tf_op jit(solution)/shard_map/reduce_scatter | solution.py:369
  426.9 266.5 %all-reduce.40.cloned.1.call-start = ((), (), s32[]{:S(2)}) async-start(), calls=%async_computation.12 | async-start | bytes 8388608 | tf_op jit(solution)/shard_map/psum | solution.py:220
  437.7 393.2 %all-reduce.38.cloned.1.call-start = ((), (), s32[]{:S(2)}) async-start(), calls=%async_computation.11 | async-start | bytes 6881280 | tf_op jit(solution)/shard_map/psum | solution.py:371
  695.5 85.8 %copy-start.19 = (bf16[2,256,1024]{2,1,0:T(8,128)(2,1)S(1)}, bf16[2,256,1024]{2,1,0:T(8,128)(2,1)}, u32[]{:S(2)}) copy-start(bf16[2,256,1024]{2,1,0:T(8,128)(2,1)} %param.38) | copy-start | bytes 3145732
  695.5 85.8 %copy-start.153 = (f32[256]{0:T(256)S(1)}, f32[256]{0:T(256)}, u32[]{:S(2)}) copy-start(f32[256]{0:T(256)} %get-tuple-element.583) | copy-start | bytes 3076
  695.5 85.8 %copy-start.154 = (f32[256]{0:T(256)S(1)}, f32[256]{0:T(256)}, u32[]{:S(2)}) copy-start(f32[256]{0:T(256)} %get-tuple-element.600) | copy-start | bytes 3076
  (164 other events, 804.8 us)
Sparse Core Ops, SparseCore 0:
  9.9 57.1 all-gather.12
  68.9 35.1 all-gather.14
  105.7 45.8 all-gather.16
  153.0 44.4 all-gather.18
  231.6 51.3 all-gather.20
  284.4 44.6 all-gather.22
  348.3 16.8 all-reduce.41
  399.3 172.9 all-reduce.35
  575.8 29.2 reduce-scatter.2
  607.9 52.6 reduce-scatter.4
  664.7 28.7 all-reduce.39
  696.4 134.3 all-reduce.37
where the time goes:
time: 853 us; the launch traced here: 844 us
  waiting for transfers between devices  405 us (47%)
  blocking collectives  129 us (15%)
  matrix products  107 us (13%)
  local copies, waits for them, and re-layouts  98.3 us (12%)
  other arithmetic  73.5 us (9%)
  between operations  20.2 us (2%)
  starting transfers between devices  10.7 us (1%)
    unnamed x13, waiting for transfers between devices  134 us
    psum x1, blocking collectives, shards(): lax.psum((grad_norm, grad_conv, grad_conv_bias, grad_dtb, grad_alog, grad...  81.7 us
    all_gather x4, waiting for transfers between devices, entering(): gathered = jax.tree.map(lambda a: lax.all_gather(a, axis), part)  80.9 us
    reduce_scatter x1, waiting for transfers between devices, shards(): lax.psum_scatter(grad_out, 'fsdp', scatter_dimension=1, tiled=True)  55.5 us
    psum x1, waiting for transfers between devices, shards(): lax.psum((grad_zx, grad_bcdt, grad_out), 'seq')  44.3 us
    dot_general x6, matrix products, ssd_span(): y_block = jnp.einsum('hts,shp->thp', mix_mat, x_heads, precision=MIXED)  32.3 us
    psum x1, waiting for transfers between devices, shards(): lax.psum(partial_out, 'head').reshape(group_size, run_rows, model_width)  31.5 us
    reduce_scatter x1, waiting for transfers between devices, shards(): lax.psum_scatter(grad_bcdt, 'fsdp', scatter_dimension=0, tiled=True)  29.1 us
  transfers between devices with their start and end apart: 16, of which 14 were waited for; matrix products, arithmetic and copies ran while one was open for 23% of the time, Pallas kernels for 0%

commit v1 on v0

v1 whole, which is shorter than its diff:
```python
import jax
import jax.numpy as jnp
from jax import lax
from jax.sharding import PartitionSpec as P

P_SIZE = 64
N = 128
NH = 32
KC = 4
NBC = 288

EPS = 1e-05
F32 = jnp.float32
BF16 = jnp.bfloat16
EXACT = lax.Precision.HIGHEST


def hop(value, axis, bit):
    return lax.ppermute(value, axis, [(i, i ^ bit) for i in range(lax.axis_size(axis))])


def step_along(value, axis, steps):
    count = lax.axis_size(axis)
    initial, last = (max(0, -steps), min(count, count - steps))
    return lax.ppermute(value, axis, [(source, source + steps) for source in range(initial, last)])


def square(axis):
    return lax.axis_size(axis) == 4


def swap_blocks(value, axis, dim):
    if not square(axis):
        return value
    place = lax.axis_index(axis)
    width = value.shape[dim] // 4
    blocks = [
        lax.dynamic_slice_in_dim(value, jnp.bitwise_xor(place, j) * width, width, dim)
        for j in range(4)
    ]
    return jnp.concatenate(blocks, axis=dim)


def gather_blocks(weight, axis):
    if not square(axis):
        gathered = lax.all_gather(weight, axis)
        return [gathered[i] for i in range(lax.axis_size(axis))]
    half = weight.shape[0] // 2
    one = hop(weight, axis, 1)
    two = hop(weight, axis, 2)
    low = hop(one[:half], axis, 2)
    high = hop(two[half:], axis, 1)
    return [weight, one, two, jnp.concatenate([low, high], axis=0)]


def scatter_blocks(blocks, axis):
    if not square(axis):
        return lax.psum_scatter(jnp.stack(blocks), axis, scatter_dimension=0, tiled=False)
    half = blocks[0].shape[0] // 2
    sent = [b.astype(BF16) for b in blocks[1:]]
    low_one = hop(jnp.concatenate([sent[0][:half], sent[2][:half]], axis=0), axis, 1)
    high_two = hop(jnp.concatenate([sent[1][half:], sent[2][half:]], axis=0), axis, 2)
    low_next = (blocks[2][:half] + low_one[half:]).astype(BF16)
    high_next = (blocks[1][half:] + high_two[half:]).astype(BF16)
    low_two = hop(low_next, axis, 2)
    high_one = hop(high_next, axis, 1)
    return jnp.concatenate(
        [
            blocks[0][:half] + low_one[:half].astype(F32) + low_two.astype(F32),
            blocks[0][half:] + high_two[:half].astype(F32) + high_one.astype(F32),
        ],
        axis=0,
    )


def sum_line(value, axis):
    if not square(axis):
        return lax.psum(value, axis)
    quarter = value.shape[0] // 4
    swapped = swap_blocks(value, axis, 0)
    own = swapped[:quarter]
    for bit in range(1, 4):
        own = own + hop(
            swapped[bit * quarter : (bit + 1) * quarter].astype(BF16), axis, bit
        ).astype(F32)
    own = own.astype(BF16)
    parts = [own] + [hop(own, axis, bit) for bit in range(1, 4)]
    return swap_blocks(jnp.concatenate(parts, axis=0), axis, 0).astype(F32)


def sum_all(value, axes):
    for axis in axes:
        count = lax.axis_size(axis)
        if count & (count - 1):
            value = lax.psum(value, axis)
            continue
        bit = 1
        while bit < count:
            value = value + hop(value, axis, bit)
            bit *= 2
    return value


def shards(
    hidden,
    segment_ids,
    norm_gain,
    w_zx,
    w_bcdt,
    conv_x,
    conv_x_bias,
    conv_bc,
    conv_bc_bias,
    dt_bias,
    a_log,
    d_skip,
    gate_gain,
    w_out,
    cotangent,
):
    head_place = lax.axis_index("head")
    seq_place = lax.axis_index("seq")
    seqs, rows, width = hidden.shape
    inner = w_zx.shape[2]
    heads = dt_bias.shape[0]
    inner_full = inner * lax.axis_size("head")
    tokens = seqs * rows
    lanes = inner + 2 * N

    seg_padded = jnp.concatenate([jnp.full((seqs, KC - 1), -1, jnp.int32), segment_ids], axis=1)
    seg_padded = jnp.concatenate([seg_padded, jnp.full((seqs, KC - 1), -2, jnp.int32)], axis=1)
    seg_wide = lax.dynamic_slice_in_dim(
        seg_padded, seq_place * rows, rows + 2 * (KC - 1), 1
    )
    seg_run = seg_wide[:, KC - 1 : KC - 1 + rows]
    seg_before = seg_wide[:, KC - 2 : KC - 1]
    head_of = jnp.arange(inner) // P_SIZE
    spread = (jnp.arange(heads)[:, None] == head_of[None, :]).astype(F32)

    def widen(v):
        return jnp.dot(v, spread, precision=EXACT)

    def per_head(v):
        return jnp.einsum("...i,hi->...h", v, spread, precision=lax.Precision.HIGH)

    hid = swap_blocks(hidden, "fsdp", 2).reshape(tokens, width).astype(F32)
    gain = swap_blocks(norm_gain, "fsdp", 0)
    cot = swap_blocks(cotangent, "fsdp", 2).reshape(tokens, width)
    inv_rms = lax.rsqrt(jnp.mean(hid * hid, axis=-1, keepdims=True) + EPS)
    normed = (hid * inv_rms * gain).astype(BF16)

    x_blocks = gather_blocks(jnp.concatenate([w_zx[:, 1], w_bcdt], axis=1), "fsdp")
    w_x = jnp.concatenate(x_blocks, axis=0)
    z_own, out_own, _ = lax.optimization_barrier((w_zx[:, 0], w_out, w_x))
    w_z = jnp.concatenate(gather_blocks(z_own, "fsdp"), axis=0)
    w_o = jnp.concatenate(gather_blocks(out_own, "fsdp"), axis=1)

    proj = jnp.dot(normed, w_x, preferred_element_type=F32).astype(BF16)
    proj = proj.reshape(seqs, rows, lanes + NH)
    xbc = proj[..., :lanes]
    dt_raw = lax.dynamic_slice_in_dim(
        proj[..., lanes:], head_place * heads, heads, 2
    ).astype(F32)
    rim = step_along(xbc[:, rows - (KC - 1) :], "seq", 1)
    ext = jnp.concatenate([rim, xbc], axis=1).astype(F32)
    taps = jnp.concatenate([conv_x, conv_bc], axis=1)
    tap_bias = jnp.concatenate([conv_x_bias, conv_bc_bias])
    same = [
        (seg_wide[:, k : k + rows] == seg_run).astype(F32)[..., None] for k in range(KC)
    ]
    pre = tap_bias
    for k in range(KC):
        pre = pre + taps[k] * ext[:, k : k + rows] * same[k]
    pre_sig = jax.nn.sigmoid(pre)
    act = (pre * pre_sig).astype(BF16)
    xs = act[..., :inner]
    bs = act[..., inner : inner + N]
    cs = act[..., inner + N :]

    dt_in = dt_raw + dt_bias
    dt = jax.nn.softplus(dt_in)
    decay = -jnp.exp(a_log)
    lower = jnp.tril(jnp.ones((rows, rows), F32))
    cum = jnp.einsum("ts,bsh->bth", lower, dt * decay, precision=EXACT)
    cum_wide, dt_wide = widen(cum), widen(dt)
    last = cum_wide[:, -1:]
    enter = (seg_run == seg_before)[..., None]
    leave = (seg_run == seg_run[:, -1:])[..., None]
    entry_gain = jnp.where(enter, jnp.exp(cum_wide), 0.0)
    tail_gain = jnp.where(leave, jnp.exp(last - cum_wide), 0.0) * dt_wide
    run_gain = jnp.where(enter[:, -1:], jnp.exp(last), 0.0).reshape(seqs, inner, 1)

    x_tail = (tail_gain * xs).astype(BF16)
    fresh = jnp.einsum("bsi,bsn->bin", x_tail, bs, preferred_element_type=F32)

    def along(own, steps):
        entering = jnp.zeros((seqs, inner, N), BF16)
        leaving = own
        for _ in range(lax.axis_size("seq") - 1):
            entering = step_along(leaving.astype(BF16), "seq", steps)
            leaving = run_gain * entering + own
        return entering, leaving

    state_in, state_out = along(fresh, 1)

    keep = jnp.tril(jnp.ones((rows, rows), bool)) & (seg_run[:, :, None] == seg_run[:, None, :])
    gap = jnp.where(keep[:, None], jnp.swapaxes(cum, 1, 2)[..., None] - jnp.swapaxes(cum, 1, 2)[:, :, None, :], 0.0)
    ldt = jnp.where(keep[:, None], jnp.exp(gap), 0.0) * jnp.swapaxes(dt, 1, 2)[:, :, None, :]
    cb = jnp.einsum("btn,bsn->bts", cs, bs, preferred_element_type=F32)
    mix = (ldt * cb[:, None]).astype(BF16)
    x_heads = xs.reshape(seqs, rows, heads, P_SIZE)
    y_block = jnp.einsum("bhts,bshp->bthp", mix, x_heads, preferred_element_type=F32).reshape(
        seqs, rows, inner
    )
    skip_wide = jnp.repeat(d_skip, P_SIZE)
    y_inter = entry_gain * jnp.einsum("btn,bin->bti", cs, state_in, preferred_element_type=F32)
    y_ssd = y_block + y_inter
    y = y_ssd + skip_wide * xs

    z = (
        jnp.dot(normed, w_z, preferred_element_type=F32)
        .astype(BF16)
        .reshape(seqs, rows, inner)
        .astype(F32)
    )
    z_sig = jax.nn.sigmoid(z)
    z_silu = z * z_sig
    gated = y * z_silu
    d_outn = jnp.einsum("td,id->ti", cot, w_o, preferred_element_type=F32).reshape(
        seqs, rows, inner
    )
    scaled = d_outn * gate_gain
    sums = jnp.stack(
        [jnp.sum(gated * gated, axis=-1), jnp.sum(scaled * gated, axis=-1)], axis=0
    )
    sums = sum_all(sums, ("head",))
    gate_rms = lax.rsqrt(sums[0] / inner_full + EPS)[..., None]
    normal = gated * gate_rms
    out_norm = (normal * gate_gain).astype(BF16).reshape(tokens, inner)
    grad_gate = jnp.sum(d_outn * normal, axis=(0, 1))
    d_gated = scaled * gate_rms - normal * (gate_rms**2 * sums[1][..., None] / inner_full)
    d_y = (d_gated * z_silu).astype(BF16)
    d_z = (d_gated * y * z_sig * (1.0 + z * (1.0 - z_sig))).astype(BF16).reshape(tokens, inner)

    dy_entry = (entry_gain * d_y).astype(BF16)
    back = jnp.einsum("bti,btn->bin", dy_entry, cs, preferred_element_type=F32)
    grad_state, _ = along(back, -1)

    mixed = sum_all(jnp.dot(out_norm, w_o, preferred_element_type=F32), ("head",))
    block_out = swap_blocks((hid + mixed).astype(BF16), "fsdp", 1).reshape(seqs, rows, width)
    grad_o = jnp.einsum("ti,td->id", out_norm, cot, preferred_element_type=F32)
    quarter = width // lax.axis_size("fsdp")
    count = lax.axis_size("fsdp")
    grad_o = scatter_blocks([grad_o[:, j * quarter : (j + 1) * quarter] for j in range(count)], "fsdp")
    grad_z = jnp.einsum("td,tc->dc", normed, d_z, preferred_element_type=F32)
    grad_z = scatter_blocks([grad_z[j * quarter : (j + 1) * quarter] for j in range(count)], "fsdp")
    grad_o = sum_line(grad_o, "seq")
    grad_z = sum_line(grad_z, "seq")

    dy_heads = d_y.reshape(seqs, rows, heads, P_SIZE)
    pair = jnp.einsum("bthp,bshp->bhts", dy_heads, x_heads, preferred_element_type=F32)
    d_cb = jnp.sum(pair * ldt, axis=1).astype(BF16)
    d_c = jnp.einsum("bts,bsn->btn", d_cb, bs, preferred_element_type=F32)
    d_b = jnp.einsum("bts,btn->bsn", d_cb, cs, preferred_element_type=F32)
    back_x = jnp.einsum("bhts,bthp->bshp", mix, dy_heads, preferred_element_type=F32).reshape(
        seqs, rows, inner
    )
    from_state = tail_gain * jnp.einsum(
        "bsn,bin->bsi", bs, grad_state, preferred_element_type=F32
    )
    d_xs = skip_wide * d_y + back_x + from_state
    d_c = d_c + jnp.einsum("bti,bin->btn", dy_entry, state_in, preferred_element_type=F32)
    d_b = d_b + jnp.einsum("bsi,bin->bsn", x_tail, grad_state, preferred_element_type=F32)

    inside = per_head(d_y * y_ssd - xs * back_x)
    outside = per_head(xs * from_state)
    through = jnp.sum(
        (run_gain * grad_state.astype(F32) * state_in).reshape(seqs, heads, P_SIZE * N), axis=-1
    )
    d_decay = (
        jnp.einsum("ts,bth->bsh", lower, inside, precision=EXACT)
        + jnp.einsum("ts,bsh->bth", lower - jnp.eye(rows), outside, precision=EXACT)
        + through[:, None]
    )
    along_x = per_head(xs * (back_x + from_state))
    dt_sig = jax.nn.sigmoid(dt_in)
    ratio = jnp.where(dt_in < -20.0, 1.0, dt_sig / jnp.maximum(dt, 1e-30))
    d_raw = along_x * ratio + decay * d_decay * dt_sig
    grad_dtb = jnp.sum(d_raw, axis=(0, 1))
    grad_alog = decay * jnp.sum(dt * d_decay, axis=(0, 1))
    grad_skip = jnp.sum(per_head(d_y * xs.astype(F32)), axis=(0, 1))

    d_raw_wide = lax.dynamic_update_slice_in_dim(
        jnp.zeros((seqs, rows, NH), F32), d_raw, head_place * heads, 2
    )
    shared = sum_all(jnp.concatenate([d_b, d_c, d_raw_wide], axis=-1), ("head",))

    d_act = jnp.concatenate([d_xs, shared[..., : 2 * N]], axis=-1)
    d_pre = d_act * pre_sig * (1.0 + pre * (1.0 - pre_sig))
    rim_back = step_along(d_pre[:, : KC - 1], "seq", -1)
    d_ext = jnp.concatenate([d_pre, rim_back], axis=1)
    d_xbc = jnp.zeros_like(d_pre)
    for k in range(KC):
        shift = KC - 1 - k
        later = seg_wide[:, KC - 1 + shift : KC - 1 + shift + rows]
        d_xbc = d_xbc + taps[k] * d_ext[:, shift : shift + rows] * (
            later == seg_run
        ).astype(F32)[..., None]
    grad_taps = jnp.stack(
        [jnp.sum(d_pre * ext[:, k : k + rows] * same[k], axis=(0, 1)) for k in range(KC)]
    )
    grad_tap_bias = jnp.sum(d_pre, axis=(0, 1))
    d_xb = jnp.concatenate([d_xbc, shared[..., 2 * N :]], axis=-1).astype(BF16)
    d_xb = d_xb.reshape(tokens, lanes + NH)

    grad_x = jnp.einsum("td,tc->dc", normed, d_xb, preferred_element_type=F32)
    grad_x = scatter_blocks([grad_x[j * quarter : (j + 1) * quarter] for j in range(count)], "fsdp")
    grad_x = sum_line(grad_x, "seq")
    by_head = jnp.einsum("tc,dc->td", d_z, w_z, preferred_element_type=F32) + jnp.einsum(
        "tc,dc->td", d_xb[:, :inner], w_x[:, :inner], preferred_element_type=F32
    )
    d_normed = sum_all(by_head, ("head",)) + jnp.einsum(
        "tc,dc->td", d_xb[:, inner:], w_x[:, inner:], preferred_element_type=F32
    )
    grad_norm = swap_blocks(jnp.sum(d_normed * hid * inv_rms, axis=0), "fsdp", 0)
    q = d_normed * gain
    grad_hidden = (
        cot.astype(F32)
        + q * inv_rms
        - hid * (inv_rms**3 * jnp.sum(q * hid, axis=-1, keepdims=True) / width)
    )
    grad_hidden = swap_blocks(grad_hidden, "fsdp", 1).reshape(seqs, rows, width)

    smalls = [grad_norm, grad_taps, grad_tap_bias, grad_dtb, grad_alog, grad_skip, grad_gate]
    flat = sum_all(jnp.concatenate([s.reshape(-1) for s in smalls]), ("fsdp", "seq"))
    summed = []
    start = 0
    for s in smalls:
        summed.append(flat[start : start + s.size].reshape(s.shape))
        start += s.size
    grad_norm, grad_taps, grad_tap_bias, grad_dtb, grad_alog, grad_skip, grad_gate = summed
    return (
        block_out,
        grad_hidden,
        grad_norm,
        jnp.stack([grad_z, grad_x[:, :inner]], axis=1),
        grad_x[:, inner:],
        grad_taps[:, :inner],
        grad_tap_bias[:inner],
        grad_taps[:, inner:],
        grad_tap_bias[inner:],
        grad_dtb,
        grad_alog,
        grad_skip,
        grad_gate,
        grad_o,
    )


def solution(mesh):
    placed = (
        P("fsdp", "seq", None),
        P("fsdp", None),
        P(),
        P("fsdp", None, "head"),
        P("fsdp", None),
        P(None, "head"),
        P("head"),
        P(),
        P(),
        P("head"),
        P("head"),
        P("head"),
        P("head"),
        P("head", "fsdp"),
        P("fsdp", "seq", None),
    )
    return jax.shard_map(
        shards,
        mesh=mesh,
        in_specs=placed,
        out_specs=(
            P("fsdp", "seq", None),
            P("fsdp", "seq", None),
            P(),
            P("fsdp", None, "head"),
            P("fsdp", None),
            P(None, "head"),
            P("head"),
            P(),
            P(),
            P("head"),
            P("head"),
            P("head"),
            P("head"),
            P("head", "fsdp"),
        ),
        check_vma=False,
    )
```

time: 853 us -> 428 us (0.50)
  waiting for transfers between devices: 405 us -> 118 us
  blocking collectives: 129 us -> 0 us
  starting transfers between devices: 10.7 us -> 90.7 us
  local copies, waits for them, and re-layouts: 98.3 us -> 63.9 us
  matrix products: 107 us -> 75.9 us
  between operations: 20.2 us -> 2.65 us
    unnamed x13 -> x0, waiting for transfers between devices: 134 us -> none
    ppermute x4 -> x58, waiting for transfers between devices: 5.69 us -> 118 us  [the longest x50 92.6 us: hop(): lax.ppermute(value, axis, [(i, i ^ bit) for i in range(lax.axis_size(axis...]
    all_gather x6 -> x0, waiting for transfers between devices: 101 us -> none  [the longest x4 80.9 us: entering(): gathered = jax.tree.map(lambda a: lax.all_gather(a, axis), part)]
    psum x4 -> x0, blocking collectives: 90.8 us -> none  [the longest x1 81.7 us: shards(): lax.psum((grad_norm, grad_conv, grad_conv_bias, grad_dtb, grad_alog, grad...]
    reduce_scatter x2 -> x0, waiting for transfers between devices: 84.6 us -> none  [the longest x1 55.5 us: shards(): lax.psum_scatter(grad_out, 'fsdp', scatter_dimension=1, tiled=True)]
    ppermute x4 -> x58, starting transfers between devices: 9.58 us -> 90.7 us  [the longest x50 69.3 us: hop(): lax.ppermute(value, axis, [(i, i ^ bit) for i in range(lax.axis_size(axis...]
    psum x3 -> x0, waiting for transfers between devices: 79.5 us -> none  [the longest x1 44.3 us: shards(): lax.psum((grad_zx, grad_bcdt, grad_out), 'seq')]
    all_gather x3 -> x0, blocking collectives: 37.9 us -> none  [the longest x1 19.8 us: shards(): lax.all_gather(w_bcdt, 'fsdp', axis=0, tiled=True)]
  transfers between devices with their start and end apart: 16 -> 58, of which waited for: 14 -> 22; matrix products, arithmetic and copies ran while one was open for 23% -> 38% of each run, Pallas kernels for 0% -> 0%
where the time goes in v1:
time: 428 us; the launch traced here: 421 us
  waiting for transfers between devices  118 us (28%)
  starting transfers between devices  90.7 us (21%)
  matrix products  75.9 us (18%)
  other arithmetic  69.8 us (16%)
  local copies, waits for them, and re-layouts  63.9 us (15%)
    ppermute x50, waiting for transfers between devices, hop(): lax.ppermute(value, axis, [(i, i ^ bit) for i in range(lax.axis_size(axis...  92.6 us
    ppermute x50, starting transfers between devices, hop(): lax.ppermute(value, axis, [(i, i ^ bit) for i in range(lax.axis_size(axis...  69.3 us
    ppermute x8, waiting for transfers between devices, step_along(): lax.ppermute(value, axis, [(source, source + steps) for source in range(i...  25.4 us
    ppermute x8, starting transfers between devices, step_along(): lax.ppermute(value, axis, [(source, source + steps) for source in range(i...  21.4 us
    unnamed x271, local copies, waits for them, and re-layouts  16.7 us
    dot_general x4, matrix products, per_head(): return jnp.einsum('...i,hi->...h', v, spread, precision=lax.Precision.HIGH)  10.5 us
  transfers between devices with their start and end apart: 58, of which 22 were waited for; matrix products, arithmetic and copies ran while one was open for 38% of the time, Pallas kernels for 0%

profile of v1, /device:TPU:0, one launch (start us, length us, event | category | flops | bytes accessed | tf_op | source)
XLA Modules:
  0.0 420.9 jit_solution(519660326089788517)
XLA Ops:
  20.5 4.5 %collective-permute-done = bf16[256,1312]{0,1:T(8,128)(2,1)} collective-permute-done((bf16[256,1312]{0,1:T(8,128)(2,1)}, bf16[256,1312]{0,1:T(8,128)(2,1)}, u32[]{:S(2)}, u32[]{:S(2)}) %collective-permute-start) | collective-permute-done | bytes 671776 | tf_op jit(solution)/shard_map/ppermute | solution.py:19
  45.8 4.6 %collective-permute-start.4 = (bf16[2,3,1280]{2,1,0:T(4,128)(2,1)S(1)}, bf16[2,3,1280]{2,1,0:T(4,128)(2,1)}, u32[]{:S(2)}, u32[]{:S(2)}) collective-permute-start(bf16[2,3,1280]{2,1,0:T(4,128)(2,1)S(1)} %copy.274), channel_id=1, source_target_pairs={{0,2},{2,4},{4,6},{1,3},{3,5},{5,7},{8,10},{10,12},{12,14},{9,11},... | collective-permute-start | bytes 46088 | tf_op jit(solution)/shard_map/ppermute | solution.py:25
  83.1 4.2 collective-permute-start.6
  87.3 4.3 %fusion.1 = f32[2,16,64,256]{3,2,1,0:T(8,128)} fusion(bf16[2,256,16,64]{1,3,2,0:T(8,128)(2,1)S(1)} %bitcast.153, f32[2,256,256]{2,1,0:T(8,128)S(1)} %fusion.138, f32[2,16,256]{2,1,0:T(8,128)S(1)} %copy-done.92, f32[2,16,256]{2,1,0:T(8,128)S(1)} %copy-done.86, pred[2,256,256]{2,1,0:T(8,128)(4,1)S(1)} %copy-done.72), kind=kOutput, calls=%fused_computation.15 | convolution fusion | flops 281018368 | bytes 3866624 | tf_op jit(solution)/shard_map/bhts,bshp->bthp/dot_general | solution.py:212
  112.6 5.0 %collective-permute-done.7 = bf16[2,1024,128]{2,1,0:T(8,128)(2,1)S(1)} collective-permute-done((bf16[2,1024,128]{2,1,0:T(8,128)(2,1)S(1)}, bf16[2,1024,128]{2,1,0:T(8,128)(2,1)S(1)}, u32[]{:S(2)}, u32[]{:S(2)}) %collective-permute-start.7) | collective-permute-done | bytes 524320 | tf_op jit(solution)/shard_map/ppermute | solution.py:25
  118.3 6.0 %multiply_reduce_fusion.7 = (f32[2,256]{1,0:T(2,128)S(1)}, f32[2,256]{1,0:T(2,128)S(1)}, f32[2,256,1024]{2,1,0:T(8,128)}, f32[2,256,1024]{2,1,0:T(8,128)}) fusion(f32[1024]{0:T(1024)S(1)} %copy-done.111, bf16[2,256,1024]{2,1,0:T(8,128)(2,1)S(1)} %bitcast.151, f32[2,256,1024]{2,1,0:T(8,128)S(1)} %multiply_add_fusion.1, ...), kind=kOutput, calls=%fused_computation.100 | convolution fusion | flops 1095760896 | bytes 11546624 | tf_op jit(solution)/shard_map/td,id->ti/dot_general | solution.py:229
  127.1 7.0 %fusion.23 = (bf16[2,256,1024]{2,1,0:T(8,128)(2,1)}, bf16[2,256,1024]{2,1,0:T(8,128)(2,1)}, bf16[2,256,1024]{2,1,0:T(8,128)(2,1)}, f32[1024]{0:T(1024)}, bf16[2,256,1024]{2,1,0:T(8,128)(2,1)}) fusion(f32[2,256,1024]{2,1,0:T(8,128)} %copy-done.4, pred[2,256]{1,0:T(4,128)(4,1)S(1)} %copy-done.102, f32[2,256]{1,0:T(2,128)S(1)} %fusion.169, ...), kind=kLoop, calls=%fused_computation.60 | loop fusion | flops 15727616 | bytes 14696960 | tf_op jit(solution)/shard_map/convert_element_type | solution.py:245
  136.4 5.7 %multiply_reduce_fusion = bf16[2,256,256]{2,1,0:T(8,128)(2,1)} fusion(f32[2,16,256]{2,1,0:T(8,128)} %fusion.188, f32[2,16,256]{2,1,0:T(8,128)} %copy-done.85, pred[2,256,256]{2,1,0:T(8,128)(4,1)} %compare_and_fusion, bf16[2,256,16,64]{1,3,2,0:T(8,128)(2,1)} %bitcast.155, bf16[2,256,16,64]{1,3,2,0:T(8,128)(2,1)} %bitcast.152), kind=kOutput, calls=%fused_computation | convolution fusion | flops 280887296 | bytes 2555904 | tf_op jit(solution)/shard_map/bthp,bshp->bhts/dot_general | solution.py:261
  142.2 4.0 fusion
  167.8 4.1 fusion.192
  177.9 7.3 %collective-permute-done.30 = bf16[256,1024]{1,0:T(8,128)(2,1)S(1)} collective-permute-done((bf16[256,1024]{1,0:T(8,128)(2,1)S(1)}, bf16[256,1024]{1,0:T(8,128)(2,1)S(1)}, u32[]{:S(2)}, u32[]{:S(2)}) %collective-permute-start.30) | collective-permute-done | bytes 524320 | tf_op jit(solution)/shard_map/ppermute | solution.py:19
  195.2 5.7 %collective-permute-done.19 = bf16[2,1024,128]{2,1,0:T(8,128)(2,1)S(1)} collective-permute-done((bf16[2,1024,128]{2,1,0:T(8,128)(2,1)S(1)}, bf16[2,1024,128]{2,1,0:T(8,128)(2,1)S(1)}, u32[]{:S(2)}, u32[]{:S(2)}) %collective-permute-start.19) | collective-permute-done | bytes 524320 | tf_op jit(solution)/shard_map/ppermute | solution.py:25
  211.8 7.4 %collective-permute-done.20 = bf16[2,1024,128]{2,1,0:T(8,128)(2,1)S(1)} collective-permute-done((bf16[2,1024,128]{2,1,0:T(8,128)(2,1)S(1)}, bf16[2,1024,128]{2,1,0:T(8,128)(2,1)S(1)}, u32[]{:S(2)}, u32[]{:S(2)}) %collective-permute-start.20) | collective-permute-done | bytes 524320 | tf_op jit(solution)/shard_map/ppermute | solution.py:25
  253.5 6.1 %collective-permute-done.36 = bf16[64,1024]{1,0:T(8,128)(2,1)S(1)} collective-permute-done((bf16[64,1024]{1,0:T(8,128)(2,1)S(1)}, bf16[64,1024]{1,0:T(8,128)(2,1)S(1)}, u32[]{:S(2)}, u32[]{:S(2)}) %collective-permute-start.36) | collective-permute-done | bytes 131104 | tf_op jit(solution)/shard_map/ppermute | solution.py:19
  266.7 4.7 %multiply_reduce_fusion.4 = (f32[1280]{0:T(1024)}, f32[1280]{0:T(1024)}, f32[1280]{0:T(1024)}, f32[1280]{0:T(1024)}, f32[1280]{0:T(1024)}, /*index=5*/f32[2,256,1280]{2,1,0:T(8,128)S(1)}) fusion(f32[2,259,1280]{2,1,0:T(8,128)S(1)} %maximum_convert_fusion, f32[2,256]{1,0:T(2,128)S(1)} %copy-done.99, f32[2,256]{1,0:T(2,128)S(1)} %copy-done.95, ...), kind=kLoop, calls=%fused_computation.38 | loop fusion | flops 13756160 | bytes 18381824 | tf_op jit(solution)/shard_map/reduce_sum | solution.py:310
  273.9 7.3 %collective-permute-done.22 = f32[2,3,1280]{2,1,0:T(4,128)S(1)} collective-permute-done((f32[2,3,1280]{2,1,0:T(4,128)S(1)}, f32[2,3,1280]{2,1,0:T(4,128)S(1)}, u32[]{:S(2)}, u32[]{:S(2)}) %collective-permute-start.22) | collective-permute-done | bytes 30752 | tf_op jit(solution)/shard_map/ppermute | solution.py:25
  305.4 7.1 %collective-permute-done.38 = bf16[256,1312]{0,1:T(8,128)(2,1)S(1)} collective-permute-done((bf16[256,1312]{0,1:T(8,128)(2,1)S(1)}, bf16[256,1312]{0,1:T(8,128)(2,1)S(1)}, u32[]{:S(2)}, u32[]{:S(2)}) %collective-permute-start.38) | collective-permute-done | bytes 671776 | tf_op jit(solution)/shard_map/ppermute | solution.py:19
  330.4 7.6 %collective-permute-done.42 = bf16[64,1312]{0,1:T(8,128)(2,1)S(1)} collective-permute-done((bf16[64,1312]{0,1:T(8,128)(2,1)S(1)}, bf16[64,1312]{0,1:T(8,128)(2,1)S(1)}, u32[]{:S(2)}, u32[]{:S(2)}) %collective-permute-start.42) | collective-permute-done | bytes 167968 | tf_op jit(solution)/shard_map/ppermute | solution.py:19
  338.0 13.5 %collective-permute-done.43 = bf16[64,1312]{0,1:T(8,128)(2,1)S(1)} collective-permute-done((bf16[64,1312]{0,1:T(8,128)(2,1)S(1)}, bf16[64,1312]{0,1:T(8,128)(2,1)S(1)}, u32[]{:S(2)}, u32[]{:S(2)}) %collective-permute-start.43) | collective-permute-done | bytes 167968 | tf_op jit(solution)/shard_map/ppermute | solution.py:19
  352.0 4.8 %collective-permute-start.45 = (bf16[64,1312]{0,1:T(8,128)(2,1)S(1)}, bf16[64,1312]{0,1:T(8,128)(2,1)S(1)}, u32[]{:S(2)}, u32[]{:S(2)}) collective-permute-start(bf16[64,1312]{0,1:T(8,128)(2,1)S(1)} %fusion.71), channel_id=1, source_target_pairs={{0,2},{2,0},{4,6},{6,4},{1,3},{3,1},{5,7},{7,5},{8,10},{10,8},{12,... | collective-permute-start | bytes 503816 | tf_op jit(solution)/shard_map/ppermute | solution.py:19
  359.9 9.2 %collective-permute-done.45 = bf16[64,1312]{0,1:T(8,128)(2,1)S(1)} collective-permute-done((bf16[64,1312]{0,1:T(8,128)(2,1)S(1)}, bf16[64,1312]{0,1:T(8,128)(2,1)S(1)}, u32[]{:S(2)}, u32[]{:S(2)}) %collective-permute-start.45) | collective-permute-done | bytes 167968 | tf_op jit(solution)/shard_map/ppermute | solution.py:19
  369.1 12.1 %collective-permute-done.46 = bf16[64,1312]{0,1:T(8,128)(2,1)S(1)} collective-permute-done((bf16[64,1312]{0,1:T(8,128)(2,1)S(1)}, bf16[64,1312]{0,1:T(8,128)(2,1)S(1)}, u32[]{:S(2)}, u32[]{:S(2)}) %collective-permute-start.46) | collective-permute-done | bytes 167968 | tf_op jit(solution)/shard_map/ppermute | solution.py:19
  388.3 5.9 %fusion.45 = (f32[1024]{0:T(1024)S(1)}, f32[512]{0:T(512)}, f32[512,1024]{1,0:T(8,128)}) fusion(f32[512]{0:T(512)S(1)} %bitcast.165, bf16[2,256,256]{2,1,0:T(8,128)(2,1)} %copy-done.35, bf16[2,256,256]{2,1,0:T(8,128)(2,1)} %copy-done.38, bf16[2,256,256]{2,1,0:T(8,128)(2,1)} %copy-done.32, bf16[2,256,256]{2,1,0:T(8,128)(2,1)} %copy-done.30, ...), kind=kOutput, calls=%fused_computation.92 | convolution fusion | flops 310966784 | bytes 9482240 | tf_op jit(solution)/shard_map/tc,dc->td/dot_general | solution.py:322
  405.4 5.5 %collective-permute-start.26 = (f32[8496]{0:T(1024)S(1)}, f32[8496]{0:T(1024)S(1)}, u32[]{:S(2)}, u32[]{:S(2)}) collective-permute-start(f32[8496]{0:T(1024)S(1)} %add.386), channel_id=1, source_target_pairs={{0,2},{2,0},{4,6},{6,4},{1,3},{3,1},{5,7},{7,5},{8,10},{10,8},{12,... | collective-permute-start | bytes 101960 | tf_op jit(solution)/shard_map/ppermute | solution.py:19
  (535 shorter events, 264.8 us)
Async XLA Ops:
  9.5 19.7 %collective-permute-start.1 = (bf16[256,1312]{0,1:T(8,128)(2,1)}, bf16[256,1312]{0,1:T(8,128)(2,1)}, u32[]{:S(2)}, u32[]{:S(2)}) collective-permute-start(bf16[256,1312]{0,1:T(8,128)(2,1)} %copy.218), channel_id=1, source_target_pairs={{0,16},{8,24},{16,0},{24,8},{1,17},{9,25},{17,1},{25,9},{2,18},{10... | collective-permute-start | bytes 2015240 | tf_op jit(solution)/shard_map/ppermute | solution.py:19
  53.3 41.2 %collective-permute-start.8 = (bf16[256,1024]{1,0:T(8,128)(2,1)S(1)}, bf16[256,1024]{1,0:T(8,128)(2,1)}, u32[]{:S(2)}, u32[]{:S(2)}) collective-permute-start(bf16[256,1024]{1,0:T(8,128)(2,1)S(1)} %bitcast.143), channel_id=1, source_target_pairs={{0,8},{8,0},{16,24},{24,16},{1,9},{9,1},{17,25},{25,17},{2,10},{10... | collective-permute-start | bytes 1572872 | tf_op jit(solution)/shard_map/ppermute | solution.py:19
  72.4 23.7 %collective-permute-start.9 = (bf16[256,1024]{1,0:T(8,128)(2,1)S(1)}, bf16[256,1024]{1,0:T(8,128)(2,1)}, u32[]{:S(2)}, u32[]{:S(2)}) collective-permute-start(bf16[256,1024]{1,0:T(8,128)(2,1)S(1)} %bitcast.145), channel_id=1, source_target_pairs={{0,16},{8,24},{16,0},{24,8},{1,17},{9,25},{17,1},{25,9},{2,18},{10... | collective-permute-start | bytes 1572872 | tf_op jit(solution)/shard_map/ppermute | solution.py:19
  72.9 25.1 %collective-permute-start.12 = (bf16[1024,256]{1,0:T(8,128)(2,1)}, bf16[1024,256]{1,0:T(8,128)(2,1)}, u32[]{:S(2)}, u32[]{:S(2)}) collective-permute-start(bf16[1024,256]{1,0:T(8,128)(2,1)} %param.28), channel_id=1, source_target_pairs={{0,8},{8,0},{16,24},{24,16},{1,9},{9,1},{17,25},{25,17},{2,10},{10... | collective-permute-start | bytes 1572872 | tf_op jit(solution)/shard_map/ppermute | solution.py:19
  73.4 27.1 %collective-permute-start.13 = (bf16[1024,256]{1,0:T(8,128)(2,1)}, bf16[1024,256]{1,0:T(8,128)(2,1)}, u32[]{:S(2)}, u32[]{:S(2)}) collective-permute-start(bf16[1024,256]{1,0:T(8,128)(2,1)} %param.28), channel_id=1, source_target_pairs={{0,16},{8,24},{16,0},{24,8},{1,17},{9,25},{17,1},{25,9},{2,18},{10... | collective-permute-start | bytes 1572872 | tf_op jit(solution)/shard_map/ppermute | solution.py:19
  83.1 23.5 %collective-permute-start.6 = (bf16[2,1024,128]{2,1,0:T(8,128)(2,1)}, bf16[2,1024,128]{2,1,0:T(8,128)(2,1)}, u32[]{:S(2)}, u32[]{:S(2)}) collective-permute-start(bf16[2,1024,128]{2,1,0:T(8,128)(2,1)} %add_convert_fusion.3), channel_id=1, source_target_pairs={{0,2},{2,4},{4,6},{1,3},{3,5},{5,7},{8,10},{10,12},{12,14},{9,11},... | collective-permute-start | bytes 1572872 | tf_op jit(solution)/shard_map/ppermute | solution.py:25
  151.9 34.7 %collective-permute-start.48 = (bf16[1024,256]{1,0:T(8,128)(2,1)}, bf16[1024,256]{1,0:T(8,128)(2,1)}, u32[]{:S(2)}, u32[]{:S(2)}) collective-permute-start(bf16[1024,256]{1,0:T(8,128)(2,1)} %pad_maximum_fusion.14), channel_id=1, source_target_pairs={{0,8},{8,0},{16,24},{24,16},{1,9},{9,1},{17,25},{25,17},{2,10},{10... | collective-permute-start | bytes 1572872 | tf_op jit(solution)/shard_map/ppermute | solution.py:19
  153.5 20.7 %collective-permute-start.50 = (bf16[1024,256]{1,0:T(8,128)(2,1)}, bf16[1024,256]{1,0:T(8,128)(2,1)}, u32[]{:S(2)}, u32[]{:S(2)}) collective-permute-start(bf16[1024,256]{1,0:T(8,128)(2,1)} %pad_maximum_fusion.15), channel_id=1, source_target_pairs={{0,16},{8,24},{16,0},{24,8},{1,17},{9,25},{17,1},{25,9},{2,18},{10... | collective-permute-start | bytes 1572872 | tf_op jit(solution)/shard_map/ppermute | solution.py:19
  155.7 19.7 %collective-permute-start.18 = (bf16[2,1024,128]{2,1,0:T(8,128)(2,1)}, bf16[2,1024,128]{2,1,0:T(8,128)(2,1)}, u32[]{:S(2)}, u32[]{:S(2)}) collective-permute-start(bf16[2,1024,128]{2,1,0:T(8,128)(2,1)} %get-tuple-element.217), channel_id=1, source_target_pairs={{2,0},{4,2},{6,4},{3,1},{5,3},{7,5},{10,8},{12,10},{14,12},{11,9},... | collective-permute-start | bytes 1572872 | tf_op jit(solution)/shard_map/ppermute | solution.py:25
  166.5 24.4 %collective-permute-start.28 = (bf16[256,1024]{1,0:T(8,128)(2,1)S(1)}, bf16[256,1024]{1,0:T(8,128)(2,1)S(1)}, u32[]{:S(2)}, u32[]{:S(2)}) collective-permute-start(bf16[256,1024]{1,0:T(8,128)(2,1)S(1)} %pad_maximum_fusion.11), channel_id=1, source_target_pairs={{0,8},{8,0},{16,24},{24,16},{1,9},{9,1},{17,25},{25,17},{2,10},{10... | collective-permute-start | bytes 1572872 | tf_op jit(solution)/shard_map/ppermute | solution.py:19
  174.2 223.2 %collective-permute-start.17 = (f32[512,1024]{1,0:T(8,128)}, f32[512,1024]{1,0:T(8,128)}, u32[]{:S(2)}, u32[]{:S(2)}) collective-permute-start(f32[512,1024]{1,0:T(8,128)} %fusion.192), channel_id=1, source_target_pairs={{0,1},{1,0},{2,3},{3,2},{4,5},{5,4},{6,7},{7,6},{8,9},{9,8},{10,11... | collective-permute-start | bytes 6291464 | tf_op jit(solution)/shard_map/ppermute | solution.py:19
  204.9 39.0 %collective-permute-start.52 = (bf16[256,256]{1,0:T(8,128)(2,1)}, bf16[256,256]{1,0:T(8,128)(2,1)}, u32[]{:S(2)}, u32[]{:S(2)}) collective-permute-start(bf16[256,256]{1,0:T(8,128)(2,1)} %get-tuple-element.155), channel_id=1, source_target_pairs={{0,2},{2,0},{4,6},{6,4},{1,3},{3,1},{5,7},{7,5},{8,10},{10,8},{12,... | collective-permute-start | bytes 393224 | tf_op jit(solution)/shard_map/ppermute | solution.py:19
  208.6 30.2 %collective-permute-start.32 = (bf16[64,1024]{1,0:T(8,128)(2,1)}, bf16[64,1024]{1,0:T(8,128)(2,1)}, u32[]{:S(2)}, u32[]{:S(2)}) collective-permute-start(bf16[64,1024]{1,0:T(8,128)(2,1)} %get-tuple-element.158), channel_id=1, source_target_pairs={{0,2},{2,0},{4,6},{6,4},{1,3},{3,1},{5,7},{7,5},{8,10},{10,8},{12,... | collective-permute-start | bytes 393224 | tf_op jit(solution)/shard_map/ppermute | solution.py:19
  208.6 31.6 %collective-permute-start.33 = (bf16[64,1024]{1,0:T(8,128)(2,1)}, bf16[64,1024]{1,0:T(8,128)(2,1)}, u32[]{:S(2)}, u32[]{:S(2)}) collective-permute-start(bf16[64,1024]{1,0:T(8,128)(2,1)} %get-tuple-element.159), channel_id=1, source_target_pairs={{0,4},{2,6},{4,0},{6,2},{1,5},{3,7},{5,1},{7,3},{8,12},{10,14},{12... | collective-permute-start | bytes 393224 | tf_op jit(solution)/shard_map/ppermute | solution.py:19
  219.2 23.5 %collective-permute-start.34 = (bf16[64,1024]{1,0:T(8,128)(2,1)}, bf16[64,1024]{1,0:T(8,128)(2,1)}, u32[]{:S(2)}, u32[]{:S(2)}) collective-permute-start(bf16[64,1024]{1,0:T(8,128)(2,1)} %get-tuple-element.160), channel_id=1, source_target_pairs={{0,6},{2,4},{4,2},{6,0},{1,7},{3,5},{5,3},{7,1},{8,14},{10,12},{12... | collective-permute-start | bytes 393224 | tf_op jit(solution)/shard_map/ppermute | solution.py:19
  242.8 20.6 %collective-permute-start.21 = (f32[2,256,288]{1,2,0:T(8,128)}, f32[2,256,288]{1,2,0:T(8,128)}, u32[]{:S(2)}, u32[]{:S(2)}) collective-permute-start(f32[2,256,288]{1,2,0:T(8,128)} %copy.245), channel_id=1, source_target_pairs={{0,1},{1,0},{2,3},{3,2},{4,5},{5,4},{6,7},{7,6},{8,9},{9,8},{10,11... | collective-permute-start | bytes 1769480 | tf_op jit(solution)/shard_map/ppermute | solution.py:19
  252.0 37.8 %collective-permute-start.55 = (bf16[256,256]{1,0:T(8,128)(2,1)}, bf16[256,256]{1,0:T(8,128)(2,1)}, u32[]{:S(2)}, u32[]{:S(2)}) collective-permute-start(bf16[256,256]{1,0:T(8,128)(2,1)} %fusion.101), channel_id=1, source_target_pairs={{0,2},{2,0},{4,6},{6,4},{1,3},{3,1},{5,7},{7,5},{8,10},{10,8},{12,... | collective-permute-start | bytes 393224 | tf_op jit(solution)/shard_map/ppermute | solution.py:19
  259.6 30.2 %collective-permute-start.56 = (bf16[256,256]{1,0:T(8,128)(2,1)}, bf16[256,256]{1,0:T(8,128)(2,1)}, u32[]{:S(2)}, u32[]{:S(2)}) collective-permute-start(bf16[256,256]{1,0:T(8,128)(2,1)} %fusion.101), channel_id=1, source_target_pairs={{0,4},{2,6},{4,0},{6,2},{1,5},{3,7},{5,1},{7,3},{8,12},{10,14},{12... | collective-permute-start | bytes 393224 | tf_op jit(solution)/shard_map/ppermute | solution.py:19
  259.6 30.2 %collective-permute-start.57 = (bf16[256,256]{1,0:T(8,128)(2,1)}, bf16[256,256]{1,0:T(8,128)(2,1)}, u32[]{:S(2)}, u32[]{:S(2)}) collective-permute-start(bf16[256,256]{1,0:T(8,128)(2,1)} %fusion.101), channel_id=1, source_target_pairs={{0,6},{2,4},{4,2},{6,0},{1,7},{3,5},{5,3},{7,1},{8,14},{10,12},{12... | collective-permute-start | bytes 393224 | tf_op jit(solution)/shard_map/ppermute | solution.py:19
  320.5 67.8 %collective-permute-start.23 = (f32[512,1024]{1,0:T(8,128)}, f32[512,1024]{1,0:T(8,128)}, u32[]{:S(2)}, u32[]{:S(2)}) collective-permute-start(f32[512,1024]{1,0:T(8,128)} %convolution_add_fusion), channel_id=1, source_target_pairs={{0,1},{1,0},{2,3},{3,2},{4,5},{5,4},{6,7},{7,6},{8,9},{9,8},{10,11... | collective-permute-start | bytes 6291464 | tf_op jit(solution)/shard_map/ppermute | solution.py:19
  327.1 24.4 %collective-permute-start.43 = (bf16[64,1312]{0,1:T(8,128)(2,1)S(1)}, bf16[64,1312]{0,1:T(8,128)(2,1)S(1)}, u32[]{:S(2)}, u32[]{:S(2)}) collective-permute-start(bf16[64,1312]{0,1:T(8,128)(2,1)S(1)} %get-tuple-element.153), channel_id=1, source_target_pairs={{0,4},{2,6},{4,0},{6,2},{1,5},{3,7},{5,1},{7,3},{8,12},{10,14},{12... | collective-permute-start | bytes 503816 | tf_op jit(solution)/shard_map/ppermute | solution.py:19
  327.1 24.4 %collective-permute-start.44 = (bf16[64,1312]{0,1:T(8,128)(2,1)S(1)}, bf16[64,1312]{0,1:T(8,128)(2,1)S(1)}, u32[]{:S(2)}, u32[]{:S(2)}) collective-permute-start(bf16[64,1312]{0,1:T(8,128)(2,1)S(1)} %get-tuple-element.154), channel_id=1, source_target_pairs={{0,6},{2,4},{4,2},{6,0},{1,7},{3,5},{5,3},{7,1},{8,14},{10,12},{12... | collective-permute-start | bytes 503816 | tf_op jit(solution)/shard_map/ppermute | solution.py:19
  356.8 24.3 %collective-permute-start.46 = (bf16[64,1312]{0,1:T(8,128)(2,1)S(1)}, bf16[64,1312]{0,1:T(8,128)(2,1)S(1)}, u32[]{:S(2)}, u32[]{:S(2)}) collective-permute-start(bf16[64,1312]{0,1:T(8,128)(2,1)S(1)} %fusion.71), channel_id=1, source_target_pairs={{0,4},{2,6},{4,0},{6,2},{1,5},{3,7},{5,1},{7,3},{8,12},{10,14},{12... | collective-permute-start | bytes 503816 | tf_op jit(solution)/shard_map/ppermute | solution.py:19
  356.8 24.3 %collective-permute-start.47 = (bf16[64,1312]{0,1:T(8,128)(2,1)S(1)}, bf16[64,1312]{0,1:T(8,128)(2,1)S(1)}, u32[]{:S(2)}, u32[]{:S(2)}) collective-permute-start(bf16[64,1312]{0,1:T(8,128)(2,1)S(1)} %fusion.71), channel_id=1, source_target_pairs={{0,6},{2,4},{4,2},{6,0},{1,7},{3,5},{5,3},{7,1},{8,14},{10,12},{12... | collective-permute-start | bytes 503816 | tf_op jit(solution)/shard_map/ppermute | solution.py:19
  (161 other events, 1634.4 us)
